TPU v7x, 32 devices: a whole 2x2x4 slice. The times are simulated.
32 devices in a mesh: tm: 1, series: 32 (over z, y, x, core).
Axes of the slice: x: 2, y: 2, z: 4, core: 2. Of those that a mesh axis runs over, the one named last changes fastest.
Arguments:
- inputs: bfloat16 [64, 512, 512], P('series', 'tm'), may hold values from -6 to 6
- cotangent: bfloat16 [64, 512, 512], P('series', 'tm'), may hold values from -6 to 6
- taps: int32 [3], replicated, may hold values from 0 to 128, as said below
- weight: float32 [1536, 512], P('series'), may hold values from -0.15625 to 0.15625
- moment_one: float32 [1536, 512], P('series'), may hold values from -10 to 10
- second_moment_state: float32 [1536, 512], P('series'), may hold values from 1 to 100
Outputs:
- grad_input: bfloat16 [64, 512, 512], P('series', 'tm')
- new_weight: float32 [1536, 512], P('series')
- new_moment_one: float32 [1536, 512], P('series')
- new_moment_two: float32 [1536, 512], P('series')
Inputs may be any that keep to these rules, and one draw needn't show every extreme that they name: taps[0] is 0, taps[2] is 128, and taps[1] lies strictly between them.
All inputs are finite; a program needn't handle non-finite values.
Results may differ from a plain program's by a relative error of at most 0.0045.
Values may be sent and summed in bfloat16 or wider, within the bound.
A program may use at most 64 MiB of HBM per device.

v0:
```python
import jax
import jax.numpy as jnp
from jax import lax
from jax.sharding import PartitionSpec as P

DILATION_GAP = 64


def passed_along(array, axis, by):
    size = lax.axis_size(axis)
    pairs = [(i, i + by) for i in range(size) if 0 <= i + by < size]
    return lax.ppermute(array, axis, pairs)


def adamw(weight, grad, moment_one, second_moment_state):
    first = 0.9 * moment_one + 0.1 * grad
    second = 0.999 * second_moment_state + 0.001 * grad * grad
    unbiased_one = first / (1.0 - 0.9**10)
    unbiased_two = second / (1.0 - 0.999**10)
    updated = weight - 0.01 * (unbiased_one / (jnp.sqrt(unbiased_two) + 1e-08) + 0.1 * weight)
    return (updated, first, second)


def body(inputs, cotangent, taps, weight, moment_one, second_moment_state):
    series_n, time_n, width = inputs.shape
    tap_count = taps.shape[0]
    receptive_span = (tap_count - 1) * DILATION_GAP
    rows = series_n * time_n
    wide = lax.all_gather(weight.astype(jnp.bfloat16), "series", axis=0, tiled=True)
    earlier = passed_along(inputs[:, time_n - receptive_span :, :], "tm", 1)
    extended = jnp.concatenate([earlier, inputs], 1)
    shifted = [
        lax.dynamic_slice_in_dim(extended, receptive_span - taps[k], time_n, 1)
        for k in range(tap_count)
    ]
    stacked = jnp.concatenate(shifted, 2).reshape(rows, tap_count * width)
    pre = jnp.dot(stacked, wide, preferred_element_type=jnp.float32)
    sig = jax.nn.sigmoid(pre)
    upstream = cotangent.reshape(rows, width)
    dpre_flat = (upstream.astype(jnp.float32) * (sig * (1.0 + pre * (1.0 - sig)))).astype(
        jnp.bfloat16
    )
    dpre = dpre_flat.reshape(series_n, time_n, width)
    ahead = passed_along(dpre[:, :receptive_span, :], "tm", -1)
    later = jnp.concatenate([dpre, ahead], 1)
    result = upstream.astype(jnp.float32)
    for k in range(tap_count):
        moved = lax.dynamic_slice_in_dim(later, taps[k], time_n, 1).reshape(rows, width)
        result = result + lax.dot_general(
            moved,
            wide[k * width : (k + 1) * width],
            (((1,), (1,)), ((), ())),
            preferred_element_type=jnp.float32,
        )
    grad_input = result.astype(jnp.bfloat16).reshape(series_n, time_n, width)
    grad_shard = lax.psum_scatter(
        lax.dot_general(
            stacked, dpre_flat, (((0,), (0,)), ((), ())), preferred_element_type=jnp.float32
        ),
        "series",
        scatter_dimension=0,
        tiled=True,
    )
    grad_shard = lax.psum(grad_shard, "tm")
    new_weight, new_moment_one, new_moment_two = adamw(
        weight, grad_shard, moment_one, second_moment_state
    )
    return (grad_input, new_weight, new_moment_one, new_moment_two)


def solution(mesh):
    in_specs = (
        P("series", "tm", None),
        P("series", "tm", None),
        P(),
        P("series", None),
        P("series", None),
        P("series", None),
    )
    out_specs = (P("series", "tm", None), P("series", None), P("series", None), P("series", None))
    return jax.shard_map(body, mesh=mesh, in_specs=in_specs, out_specs=out_specs, check_vma=False)
```

profile of v0, /device:TPU:0, one launch (start us, length us, event | category | flops | bytes accessed | tf_op | source)
XLA Modules:
  0.0 186.7 jit_solution(17833757055605146597)
XLA Ops:
  7.2 0.0 all-gather.2.cloned.1.call-start
  7.2 1.5 convert_element_type.18
  8.7 0.0 all-gather.2.cloned.1.call-update
  8.8 0.0 reduce-scatter.2.cloned.1.call-start
  8.8 1.0 slice.27
  9.8 0.7 collective-permute-start
  10.5 1.4 fusion.14
  15.7 1.3 constant_dynamic-update-slice_fusion
  17.0 0.8 constant_dynamic-slice_fusion.2
  17.9 0.3 pad_maximum_fusion
  18.1 51.0 %all-gather.2.cloned.1.call-done = bf16[1536,512]{1,0:T(8,128)(2,1)} async-done(((bf16[48,512]{1,0:T(8,128)(2,1)}), bf16[1536,512]{1,0:T(8,128)(2,1)}) %all-gather.2.cloned.1.call-update) | async-done | bytes 1572880 | tf_op jit(solution)/shard_map/all_gather | solution.py:29
  69.1 4.0 %fusion = bf16[1024,512]{1,0:T(8,128)(2,1)S(1)} fusion(bf16[2,512,512]{2,1,0:T(8,128)(2,1)} %param.7, bf16[1024,1536]{1,0:T(8,128)(2,1)S(1)} %bitcast.22, bf16[1536,512]{1,0:T(8,128)(2,1)} %all-gather.2.cloned.1.call-done), kind=kOutput, calls=%fused_computation.3 | convolution fusion | flops 1615855616 | bytes 6815744 | tf_op jit(solution)/shard_map/dot_general | solution.py:37
  73.2 1.0 copy-done
  74.1 3.5 %fusion.15 = f32[1536,512]{1,0:T(8,128)} fusion(bf16[1024,1536]{1,0:T(8,128)(2,1)S(1)} %bitcast.23, bf16[1024,512]{1,0:T(8,128)(2,1)S(1)} %fusion), kind=kOutput, calls=%fused_computation.31 | convolution fusion | flops 1610612736 | bytes 7340032 | tf_op jit(solution)/shard_map/dot_general | solution.py:57
  77.6 0.0 reduce-scatter.2.cloned.1.call-update
  77.6 1.2 copy-done.1
  78.9 0.7 collective-permute-start.1
  85.4 3.1 %fusion.4 = (bf16[2,512,512]{2,1,0:T(8,128)(2,1)S(1)}, bf16[2,512,512]{2,1,0:T(8,128)(2,1)S(1)}, bf16[2,512,512]{2,1,0:T(8,128)(2,1)S(1)}) fusion(s32[]{:T(128)S(6)} %select_n.23, bf16[2,512,512]{2,1,0:T(8,128)(2,1)S(1)} %bitcast.25, bf16[2,128,512]{2,1,0:T(8,128)(2,1)S(1)} %collective-permute-done.1, s32[]{:T(128)S(6)} %select_n.21, s32[]{:T(128)S(6)} %select_n.22), kind=kLoop, calls=%fused_computation.13 | loop fusion | flops 6291456 | bytes 4456460 | tf_op jit(solution)/shard_map/concatenate | solution.py:45
  88.4 0.7 fusion.10
  89.2 0.7 fusion.8
  89.9 0.5 copy-done.3
  90.4 1.8 fusion.3
  92.2 86.0 %reduce-scatter.2.cloned.1.call-done = f32[48,512]{1,0:T(8,128)} async-done(((f32[1536,512]{1,0:T(8,128)}), f32[48,512]{1,0:T(8,128)}) %reduce-scatter.2.cloned.1.call-update) | async-done | bytes 98320 | tf_op jit(solution)/shard_map/reduce_scatter | solution.py:56
  178.2 1.6 multiply_subtract_fusion
  (15 shorter events, 0.1 us)
Async XLA Ops:
  7.2 61.9 %all-gather.2.cloned.1.call-start = ((), (), s32[]{:S(2)}) async-start(), calls=%async_computation.1 | async-start | bytes 1622016 | tf_op jit(solution)/shard_map/all_gather | solution.py:29
  8.8 169.4 %reduce-scatter.2.cloned.1.call-start = ((), (), s32[]{:S(2)}) async-start(), calls=%async_computation.2 | async-start | bytes 3244032 | tf_op jit(solution)/shard_map/reduce_scatter | solution.py:56
  9.8 5.9 %collective-permute-start = (bf16[2,128,512]{2,1,0:T(8,128)(2,1)S(1)}, bf16[2,128,512]{2,1,0:T(8,128)(2,1)S(1)}, u32[]{:S(2)}, u32[]{:S(2)}) collective-permute-start(bf16[2,128,512]{2,1,0:T(8,128)(2,1)S(1)} %slice.27), channel_id=1, source_target_pairs={} | collective-permute-start | bytes 786440 | tf_op jit(solution)/shard_map/ppermute | solution.py:12
  73.2 1.0 copy-start
  77.6 1.2 copy-start.1
  78.9 6.5 %collective-permute-start.1 = (bf16[2,128,512]{2,1,0:T(8,128)(2,1)S(1)}, bf16[2,128,512]{2,1,0:T(8,128)(2,1)S(1)}, u32[]{:S(2)}, u32[]{:S(2)}) collective-permute-start(bf16[2,128,512]{2,1,0:T(8,128)(2,1)S(1)} %slice.35), channel_id=1, source_target_pairs={} | collective-permute-start | bytes 786440 | tf_op jit(solution)/shard_map/ppermute | solution.py:12
  85.3 3.1 %copy-start.2 = (bf16[1536,512]{1,0:T(8,128)(2,1)S(1)}, bf16[1536,512]{1,0:T(8,128)(2,1)}, u32[]{:S(2)}) copy-start(bf16[1536,512]{1,0:T(8,128)(2,1)} %all-gather.2.cloned.1.call-done) | copy-start | bytes 4718596
  89.2 1.2 copy-start.3
  90.4 87.8 %copy-start.4 = (f32[48,512]{1,0:T(8,128)S(1)}, f32[48,512]{1,0:T(8,128)}, u32[]{:S(2)}) copy-start(f32[48,512]{1,0:T(8,128)} %param.9) | copy-start | bytes 294916
  90.4 87.8 %copy-start.5 = (f32[48,512]{1,0:T(8,128)S(1)}, f32[48,512]{1,0:T(8,128)}, u32[]{:S(2)}) copy-start(f32[48,512]{1,0:T(8,128)} %param.10) | copy-start | bytes 294916
  90.4 87.8 %copy-start.6 = (f32[48,512]{1,0:T(8,128)S(1)}, f32[48,512]{1,0:T(8,128)}, u32[]{:S(2)}) copy-start(f32[48,512]{1,0:T(8,128)} %param.11) | copy-start | bytes 294916
Sparse Core Ops, SparseCore 0:
  11.4 57.6 all-gather.1
  77.8 100.3 reduce-scatter.1
where the time goes:
time: 187 us
  waiting for transfers between devices  137 us (73%)
  between operations  23.8 us (13%)
  matrix products  10.8 us (6%)
  local copies, waits for them, and re-layouts  7.16 us (4%)
  other arithmetic  6.47 us (3%)
    reduce_scatter x1, waiting for transfers between devices, body(): lax.psum_scatter(lax.dot_general(stacked, dpre_flat, (((0,), (0,)), ((),...  86 us
    all_gather x1, waiting for transfers between devices, body(): lax.all_gather(weight.astype(jnp.bfloat16), 'series', axis=0, tiled=True)  51 us
    dot_general x1, matrix products, body(): pre = jnp.dot(stacked, wide, preferred_element_type=jnp.float32)  4.04 us
  transfers between devices with their start and end apart: 4, of which 2 were waited for; matrix products, arithmetic and copies ran while one was open for 6% of the time, Pallas kernels for 0%

commit v1 on v0

--- a/solution.py
+++ b/solution.py
@@ -1,6 +1,10 @@
+import functools
+
 import jax
 import jax.numpy as jnp
 from jax import lax
+from jax.experimental import pallas as pl
+from jax.experimental.pallas import tpu as pltpu
 from jax.sharding import PartitionSpec as P
 
 DILATION_GAP = 64
@@ -68,6 +72,274 @@
     return (grad_input, new_weight, new_moment_one, new_moment_two)
 
 
+MESH = pl.DeviceIdType.MESH
+F32, BF16 = jnp.float32, jnp.bfloat16
+PLANES, IN_PLANE = 4, 8
+
+
+def fits(mesh):
+    return mesh.shape["tm"] == 1 and mesh.shape["series"] == PLANES * IN_PLANE
+
+
+def matmul(a, b):
+    return jnp.dot(a, b, preferred_element_type=F32)
+
+
+def matmul_t(a, b):
+    return lax.dot_general(a, b, (((1,), (1,)), ((), ())), preferred_element_type=F32)
+
+
+def kernel(
+    taps_ref, x_hbm, cot_hbm, w_hbm, m1_hbm, m2_hbm,
+    gi_hbm, nw_hbm, n1_hbm, n2_hbm,
+    x, cot, w, m1, m2, gi, nw, n1, n2,
+    wide, xs, xt, dk, g, s1, r1, s2a, s2b, r2a, r2b, s3a, s3b, r3a, r3b, s4, r4,
+    load_sem, store_sem, ag_send, ag_recv, rs_send, rs_recv,
+):
+    series_n, time_n, width = x.shape
+    span = 2 * DILATION_GAP
+    rows = w.shape[0]
+    half = width // 2
+    tm = lax.axis_index("tm")
+    me = lax.axis_index("series")
+    core = lax.rem(me, 2)
+    px_i = lax.rem(me // 2, 2)
+    py_i = lax.rem(me // 4, 2)
+    z = me // IN_PLANE
+
+    def index(zz, yy, xx, cc):
+        return ((zz * 2 + yy) * 2 + xx) * 2 + cc
+
+    def block(zz, yy, xx, cc):
+        return pl.ds(pl.multiple_of(index(zz, yy, xx, cc) * rows, 16), rows)
+
+    to_x = (tm, index(z, py_i, 1 - px_i, core))
+    to_y = (tm, index(z, 1 - py_i, px_i, core))
+    to_c = (tm, index(z, py_i, px_i, 1 - core))
+    to_z = [None] + [(tm, index(lax.rem(z + d, PLANES), py_i, px_i, core)) for d in (1, 2, 3)]
+
+    loads = [
+        pltpu.make_async_copy(src, dst, load_sem.at[i])
+        for i, (src, dst) in enumerate(
+            [(w_hbm, w), (x_hbm, x), (cot_hbm, cot), (m1_hbm, m1), (m2_hbm, m2)]
+        )
+    ]
+    for c in loads:
+        c.start()
+
+    barrier = pltpu.get_barrier_semaphore()
+    for dev in (to_x, to_y, to_c, *to_z[1:]):
+        pl.semaphore_signal(barrier, inc=1, device_id=dev, device_id_type=MESH)
+
+    loads[0].wait()
+    own = block(z, py_i, px_i, core)
+    wide[own, :] = w[...].astype(BF16)
+    pl.semaphore_wait(barrier, 6)
+
+    def start(src, dst, sems, k, dev):
+        c = pltpu.make_async_remote_copy(
+            src_ref=src, dst_ref=dst, send_sem=sems[0].at[k], recv_sem=sems[1].at[k],
+            device_id=dev, device_id_type=MESH,
+        )
+        c.start()
+        return c
+
+    ag = (ag_send, ag_recv)
+    rs = (rs_send, rs_recv)
+    A, B, ALL = pl.ds(0, half), pl.ds(half, half), pl.ds(0, width)
+
+    def pass_on(blk, cols, k, dev):
+        return start(wide.at[blk, cols], wide.at[blk, cols], ag, k, dev)
+
+    sent = []
+    z_copies = [None] + [pass_on(own, ALL, d, to_z[d]) for d in (1, 2, 3)]
+    sent += z_copies[1:]
+    x1, y1 = [], []
+    for j in range(PLANES):
+        zj = lax.rem(z + PLANES - j, PLANES)
+        if j:
+            z_copies[j].wait_recv()
+        blk = block(zj, py_i, px_i, core)
+        x1.append(pass_on(blk, ALL, 4 + j, to_x))
+        y1.append(pass_on(blk, ALL, 8 + j, to_y))
+        sent.append(pass_on(blk, ALL, 12 + j, to_c))
+        if j == 0:
+            loads[1].wait()
+            tap = taps_ref[1]
+            row = lax.broadcasted_iota(jnp.int32, (time_n, time_n), 0)
+            column = lax.broadcasted_iota(jnp.int32, (time_n, time_n), 1)
+            back = jnp.where(column == row - tap, 1.0, 0.0).astype(BF16)
+            for s in range(series_n):
+                at = pl.ds(s * time_n, time_n)
+                xs[0, at, :] = x[s]
+                xs[1, at, :] = matmul(back, x[s]).astype(BF16)
+                xs[2, pl.ds(s * time_n, span), :] = jnp.zeros((span, width), BF16)
+                xs[2, pl.ds(s * time_n + span, time_n - span), :] = x[s, pl.ds(0, time_n - span), :]
+                for k in range(3):
+                    xt[k, :, at] = xs[k, at, :].T
+    x2, y2 = [], []
+    c_in = list(sent[3:])
+    for j in range(PLANES):
+        zj = lax.rem(z + PLANES - j, PLANES)
+        x1[j].wait_recv()
+        blk = block(zj, py_i, 1 - px_i, core)
+        y2.append(pass_on(blk, A, 16 + j, to_y))
+        c_in.append(pass_on(blk, ALL, 20 + j, to_c))
+        y1[j].wait_recv()
+        blk = block(zj, 1 - py_i, px_i, core)
+        x2.append(pass_on(blk, B, 24 + j, to_x))
+        c_in.append(pass_on(blk, ALL, 28 + j, to_c))
+    for j in range(PLANES):
+        zj = lax.rem(z + PLANES - j, PLANES)
+        y2[j].wait_recv()
+        x2[j].wait_recv()
+        c_in.append(pass_on(block(zj, 1 - py_i, 1 - px_i, core), ALL, 32 + j, to_c))
+    for c in c_in:
+        c.wait_recv()
+
+    loads[2].wait()
+    for s in range(series_n):
+        at = pl.ds(s * time_n, time_n)
+        pre = matmul(xs[0, at, :], wide[pl.ds(0, width), :])
+        for k in (1, 2):
+            pre = pre + matmul(xs[k, at, :], wide[pl.ds(k * width, width), :])
+        sig = jax.nn.sigmoid(pre)
+        dk[0, at, :] = (cot[s].astype(F32) * (sig * (1.0 + pre * (1.0 - sig)))).astype(BF16)
+
+    c1 = []
+    for k in range(3):
+        g[pl.ds(k * width, width), :] = matmul(xt[k], dk[0])
+        for zz in ((0,), (1,), (2, 3))[k]:
+            for q in range(4):
+                s1[zz, q] = g[block(zz, q // 2, q % 2, 1 - core), :].astype(BF16)
+            c1.append(start(s1.at[zz], r1.at[zz], rs, zz, to_c))
+
+    ahead = jnp.where(column == row + tap, 1.0, 0.0).astype(BF16)
+
+    def grad_input(s):
+        total = cot[s].astype(F32)
+        first = s * time_n
+        dk[1, pl.ds(first, time_n), :] = matmul(ahead, dk[0, pl.ds(first, time_n), :]).astype(BF16)
+        dk[2, pl.ds(first, time_n - span), :] = dk[0, pl.ds(first + span, time_n - span), :]
+        dk[2, pl.ds(first + time_n - span, span), :] = jnp.zeros((span, width), BF16)
+        for k in range(3):
+            total = total + matmul_t(dk[k, pl.ds(s * time_n, time_n), :], wide[pl.ds(k * width, width), :])
+        gi[s] = total.astype(BF16)
+        c = pltpu.make_async_copy(gi.at[s], gi_hbm.at[s], store_sem.at[s])
+        c.start()
+        return c
+
+    order = (2, 1, 3, 0)
+    a2, b2, a3, b3, z4 = {}, {}, {}, {}, {}
+    for c in c1:
+        c.wait_recv()
+    for d in order:
+        zz = lax.rem(z + d, PLANES)
+
+        def both(yy, xx, cols):
+            return g[block(zz, yy, xx, core), cols] + r1[zz, yy * 2 + xx, :, cols].astype(F32)
+
+        for q in range(2):
+            s2a[d, q] = both(q, 1 - px_i, A).astype(BF16)
+            s2b[d, q] = both(1 - py_i, q, B).astype(BF16)
+        a2[d] = start(s2a.at[d], r2a.at[d], rs, 4 + d, to_x)
+        b2[d] = start(s2b.at[d], r2b.at[d], rs, 8 + d, to_y)
+    stores = [grad_input(0)]
+    for d in order:
+        zz = lax.rem(z + d, PLANES)
+        a2[d].wait_recv()
+        other = 1 - py_i
+        s3a[d] = (
+            g[block(zz, other, px_i, core), A] + r1[zz, other * 2 + px_i, :, A].astype(F32)
+            + r2a[d, other].astype(F32)
+        ).astype(BF16)
+        a3[d] = start(s3a.at[d], r3a.at[d], rs, 12 + d, to_y)
+        b2[d].wait_recv()
+        other = 1 - px_i
+        s3b[d] = (
+            g[block(zz, py_i, other, core), B] + r1[zz, py_i * 2 + other, :, B].astype(F32)
+            + r2b[d, other].astype(F32)
+        ).astype(BF16)
+        b3[d] = start(s3b.at[d], r3b.at[d], rs, 16 + d, to_x)
+    stores += [grad_input(s) for s in range(1, series_n)]
+    grad = None
+    for d in order:
+        zz = lax.rem(z + d, PLANES)
+        mine = block(zz, py_i, px_i, core)
+        q = py_i * 2 + px_i
+        a3[d].wait_recv()
+        b3[d].wait_recv()
+        sum_a = g[mine, A] + r1[zz, q, :, A].astype(F32) + r2a[d, py_i].astype(F32) + r3a[d].astype(F32)
+        sum_b = g[mine, B] + r1[zz, q, :, B].astype(F32) + r2b[d, px_i].astype(F32) + r3b[d].astype(F32)
+        if d:
+            s4[d - 1, :, A] = sum_a.astype(BF16)
+            s4[d - 1, :, B] = sum_b.astype(BF16)
+            z4[d] = start(s4.at[d - 1], r4.at[d - 1], rs, 19 + d, to_z[d])
+        else:
+            grad = jnp.concatenate([sum_a, sum_b], 1)
+    loads[3].wait()
+    loads[4].wait()
+    for d in (1, 2, 3):
+        z4[d].wait_recv()
+        grad = grad + r4[d - 1].astype(F32)
+    nw[...], n1[...], n2[...] = adamw(w[...], grad, m1[...], m2[...])
+    for i, (src, dst) in enumerate([(nw, nw_hbm), (n1, n1_hbm), (n2, n2_hbm)]):
+        c = pltpu.make_async_copy(src, dst, store_sem.at[series_n + i])
+        c.start()
+        stores.append(c)
+    for c in z_copies[1:] + x1 + y1 + x2 + y2 + c_in + c1:
+        c.wait_send()
+    for group in (a2, b2, a3, b3, z4):
+        for c in group.values():
+            c.wait_send()
+    for c in stores:
+        c.wait()
+
+
+def fused(inputs, cotangent, taps, weight, moment_one, second_moment_state):
+    series_n, time_n, width = inputs.shape
+    rows = weight.shape[0]
+    span = (taps.shape[0] - 1) * DILATION_GAP
+    depth = taps.shape[0] * width
+    half = width // 2
+    flat = series_n * time_n
+    state = jax.ShapeDtypeStruct(weight.shape, F32)
+    hbm = pl.BlockSpec(memory_space=pl.ANY)
+    V = pltpu.VMEM
+    return tuple(pl.pallas_call(
+        kernel,
+        out_shape=[jax.ShapeDtypeStruct(inputs.shape, BF16), state, state, state],
+        in_specs=[pl.BlockSpec(memory_space=pltpu.SMEM)] + [hbm] * 5,
+        out_specs=[hbm] * 4,
+        scratch_shapes=[
+            V(inputs.shape, BF16), V(inputs.shape, BF16),
+            V(weight.shape, F32), V(weight.shape, F32), V(weight.shape, F32),
+            V(inputs.shape, BF16),
+            V(weight.shape, F32), V(weight.shape, F32), V(weight.shape, F32),
+            V((depth, width), BF16),
+            V((3, flat, width), BF16),
+            V((3, width, flat), BF16),
+            V((3, flat, width), BF16),
+            V((depth, width), F32),
+            V((PLANES, 4, rows, width), BF16), V((PLANES, 4, rows, width), BF16),
+            V((PLANES, 2, rows, half), BF16), V((PLANES, 2, rows, half), BF16),
+            V((PLANES, 2, rows, half), BF16), V((PLANES, 2, rows, half), BF16),
+            V((PLANES, rows, half), BF16), V((PLANES, rows, half), BF16),
+            V((PLANES, rows, half), BF16), V((PLANES, rows, half), BF16),
+            V((3, rows, width), BF16), V((3, rows, width), BF16),
+            pltpu.SemaphoreType.DMA((5,)), pltpu.SemaphoreType.DMA((series_n + 3,)),
+            pltpu.SemaphoreType.DMA((36,)), pltpu.SemaphoreType.DMA((36,)),
+            pltpu.SemaphoreType.DMA((23,)), pltpu.SemaphoreType.DMA((23,)),
+        ],
+        compiler_params=pltpu.CompilerParams(
+            collective_id=0, has_side_effects=True, vmem_limit_bytes=48 * 1024 * 1024
+        ),
+        cost_estimate=pl.CostEstimate(
+            flops=6 * flat * depth * width, bytes_accessed=6 * flat * width, transcendentals=flat * width
+        ),
+    )(taps, inputs, cotangent, weight, moment_one, second_moment_state))
+
+
 def solution(mesh):
     in_specs = (
         P("series", "tm", None),
@@ -78,4 +350,5 @@
         P("series", None),
     )
     out_specs = (P("series", "tm", None), P("series", None), P("series", None), P("series", None))
-    return jax.shard_map(body, mesh=mesh, in_specs=in_specs, out_specs=out_specs, check_vma=False)
+    step = fused if fits(mesh) else body
+    return jax.shard_map(step, mesh=mesh, in_specs=in_specs, out_specs=out_specs, check_vma=False)

time: 187 us -> 49.1 us (0.26)
  waiting for transfers between devices: 137 us -> 0 us
  Pallas kernels: 0 us -> 39.5 us
  between operations: 23.8 us -> 0.66 us
  matrix products: 10.8 us -> 0 us
  other arithmetic: 6.47 us -> 0 us
    reduce_scatter x1 -> x0, waiting for transfers between devices: 86 us -> none  [body(): lax.psum_scatter(lax.dot_general(stacked, dpre_flat, (((0,), (0,)), ((),...]
    all_gather x1 -> x0, waiting for transfers between devices: 51 us -> none  [body(): lax.all_gather(weight.astype(jnp.bfloat16), 'series', axis=0, tiled=True)]
    pallas_call x0 -> x1, Pallas kernels: none -> 39.5 us  [fused(): pl.pallas_call(kernel, out_shape=[jax.ShapeDtypeStruct(inputs.shape, BF16...]
    dot_general x5 -> x0, matrix products: 10.8 us -> none  [the longest x1 4.04 us: body(): pre = jnp.dot(stacked, wide, preferred_element_type=jnp.float32)]
    unnamed x15 -> x16, local copies, waits for them, and re-layouts: 2.69 us -> 8.67 us
    concatenate x2 -> x0, other arithmetic: 3.31 us -> none  [the longest x1 3.05 us: body(): later = jnp.concatenate([dpre, ahead], 1)]
    slice x3 -> x0, local copies, waits for them, and re-layouts: 2.37 us -> none  [the longest x1 1.38 us: body(): taps[k]]
  transfers between devices with their start and end apart: 4 -> 0, of which waited for: 2 -> 0; matrix products, arithmetic and copies ran while one was open for 6% -> 0% of each run, Pallas kernels for 0% -> 0%
where the time goes in v1:
time: 49.1 us; the launch traced here: 48.8 us
  Pallas kernels  39.5 us (80%)
  local copies, waits for them, and re-layouts  8.67 us (18%)
  between operations  0.66 us (1%)
    pallas_call x1, Pallas kernels, fused(): pl.pallas_call(kernel, out_shape=[jax.ShapeDtypeStruct(inputs.shape, BF16...  39.5 us
    unnamed x16, local copies, waits for them, and re-layouts  8.67 us

profile of v1, /device:TPU:0, one launch (start us, length us, event | category | flops | bytes accessed | tf_op | source)
XLA Modules:
  0.0 48.8 jit_solution(17524498029822380598)
XLA Ops:
  0.6 0.0 copy-start
  0.6 1.2 %copy-done = bf16[2,512,512]{2,1,0:T(8,128)(2,1)S(1)} copy-done((bf16[2,512,512]{2,1,0:T(8,128)(2,1)S(1)}, bf16[2,512,512]{2,1,0:T(8,128)(2,1)}, u32[]{:S(2)}) %copy-start) | copy-done | bytes 1048600
  1.9 0.0 copy-start.1
  1.9 1.2 %copy-done.1 = bf16[2,512,512]{2,1,0:T(8,128)(2,1)S(1)} copy-done((bf16[2,512,512]{2,1,0:T(8,128)(2,1)S(1)}, bf16[2,512,512]{2,1,0:T(8,128)(2,1)}, u32[]{:S(2)}) %copy-start.1) | copy-done | bytes 1048600
  3.1 0.0 copy-start.2
  3.1 0.9 %copy-done.2 = f32[48,512]{1,0:T(8,128)S(1)} copy-done((f32[48,512]{1,0:T(8,128)S(1)}, f32[48,512]{1,0:T(8,128)}, u32[]{:S(2)}) %copy-start.2) | copy-done | bytes 98328
  4.0 0.0 copy-start.3
  4.0 0.9 %copy-done.3 = f32[48,512]{1,0:T(8,128)S(1)} copy-done((f32[48,512]{1,0:T(8,128)S(1)}, f32[48,512]{1,0:T(8,128)}, u32[]{:S(2)}) %copy-start.3) | copy-done | bytes 98328
  4.9 0.0 copy-start.4
  4.9 0.9 %copy-done.4 = f32[48,512]{1,0:T(8,128)S(1)} copy-done((f32[48,512]{1,0:T(8,128)S(1)}, f32[48,512]{1,0:T(8,128)}, u32[]{:S(2)}) %copy-start.4) | copy-done | bytes 98328
  5.8 0.0 copy-start.5
  5.8 0.7 %copy-done.5 = s32[3]{0:T(128)S(1)} copy-done((s32[3]{0:T(128)S(1)}, s32[3]{0:T(128)}, u32[]{:S(2)}) %copy-start.5) | copy-done | bytes 36
  6.4 39.5 %shard_map.93 = (bf16[2,512,512]{2,1,0:T(8,128)(2,1)S(1)}, f32[48,512]{1,0:T(8,128)S(1)}, f32[48,512]{1,0:T(8,128)S(1)}, f32[48,512]{1,0:T(8,128)S(1)}) custom-call(s32[3]{0:T(128)S(1)} %copy-done.5, bf16[2,512,512]{2,1,0:T(8,128)(2,1)S(1)} %copy-done, bf16[2,512,512]{2,1,0:T(8,128)(2,1)S(1)} %copy-done.1, f32[48,512]{1,0:T(8,128)S(1)} %copy-done.2, ...), custom_call_target="tpu_custom_call" | custom-call | flops 4831838208 | bytes 3145728 | tf_op jit(solution)/shard_map/pallas_call | solution.py:309
  45.9 1.0 %copy.14 = bf16[2,512,512]{2,1,0:T(8,128)(2,1)} copy(bf16[2,512,512]{2,1,0:T(8,128)(2,1)S(1)} %get-tuple-element.8) | data formatting | bytes 2097152
  46.9 0.6 %copy.15 = f32[48,512]{1,0:T(8,128)} copy(f32[48,512]{1,0:T(8,128)S(1)} %get-tuple-element.9) | data formatting | bytes 196608
  47.5 0.6 %copy.16 = f32[48,512]{1,0:T(8,128)} copy(f32[48,512]{1,0:T(8,128)S(1)} %get-tuple-element.10) | data formatting | bytes 196608
  48.2 0.6 %copy.17 = f32[48,512]{1,0:T(8,128)} copy(f32[48,512]{1,0:T(8,128)S(1)} %get-tuple-element.11) | data formatting | bytes 196608
Async XLA Ops:
  0.6 1.2 %copy-start = (bf16[2,512,512]{2,1,0:T(8,128)(2,1)S(1)}, bf16[2,512,512]{2,1,0:T(8,128)(2,1)}, u32[]{:S(2)}) copy-start(bf16[2,512,512]{2,1,0:T(8,128)(2,1)} %x_hbm.1) | copy-start | bytes 3145732
  1.9 1.2 %copy-start.1 = (bf16[2,512,512]{2,1,0:T(8,128)(2,1)S(1)}, bf16[2,512,512]{2,1,0:T(8,128)(2,1)}, u32[]{:S(2)}) copy-start(bf16[2,512,512]{2,1,0:T(8,128)(2,1)} %cot_hbm.1) | copy-start | bytes 3145732
  3.1 0.9 %copy-start.2 = (f32[48,512]{1,0:T(8,128)S(1)}, f32[48,512]{1,0:T(8,128)}, u32[]{:S(2)}) copy-start(f32[48,512]{1,0:T(8,128)} %w_hbm.1) | copy-start | bytes 294916
  4.0 0.9 %copy-start.3 = (f32[48,512]{1,0:T(8,128)S(1)}, f32[48,512]{1,0:T(8,128)}, u32[]{:S(2)}) copy-start(f32[48,512]{1,0:T(8,128)} %m1_hbm.1) | copy-start | bytes 294916
  4.9 0.9 %copy-start.4 = (f32[48,512]{1,0:T(8,128)S(1)}, f32[48,512]{1,0:T(8,128)}, u32[]{:S(2)}) copy-start(f32[48,512]{1,0:T(8,128)} %m2_hbm.1) | copy-start | bytes 294916
  5.8 0.7 %copy-start.5 = (s32[3]{0:T(128)S(1)}, s32[3]{0:T(128)}, u32[]{:S(2)}) copy-start(s32[3]{0:T(128)} %taps_ref.1) | copy-start | bytes 40

commit v2 on v0

--- a/solution.py
+++ b/solution.py
@@ -1,6 +1,10 @@
+import functools
+
 import jax
 import jax.numpy as jnp
 from jax import lax
+from jax.experimental import pallas as pl
+from jax.experimental.pallas import tpu as pltpu
 from jax.sharding import PartitionSpec as P
 
 DILATION_GAP = 64
@@ -68,6 +72,336 @@
     return (grad_input, new_weight, new_moment_one, new_moment_two)
 
 
+MESH = pl.DeviceIdType.MESH
+F32, BF16 = jnp.float32, jnp.bfloat16
+PLANES, IN_PLANE = 4, 8
+
+
+def fits(mesh):
+    return mesh.shape["tm"] == 1 and mesh.shape["series"] == PLANES * IN_PLANE
+
+
+def matmul(a, b):
+    return jnp.dot(a, b, preferred_element_type=F32)
+
+
+def matmul_t(a, b):
+    return lax.dot_general(a, b, (((1,), (1,)), ((), ())), preferred_element_type=F32)
+
+
+def kernel(
+    taps_ref, x_hbm, cot_hbm, w_hbm, gi_hbm, grad_hbm,
+    x, cot, w, gi, grad_ref,
+    wide, xs, xt, pre, dk, g, s1, r1, s2a, s2b, r2a, r2b, s3a, s3b, r3a, r3b, s4, r4,
+    load_sem, store_sem, ag_send, ag_recv, rs_send, rs_recv,
+):
+    series_n, time_n, width = x.shape
+    flat = series_n * time_n
+    span = 2 * DILATION_GAP
+    rows = w.shape[0]
+    group = IN_PLANE * rows
+    half = width // 2
+    tm = lax.axis_index("tm")
+    me = lax.axis_index("series")
+    core = lax.rem(me, 2)
+    px = lax.rem(me // 2, 2)
+    py = lax.rem(me // 4, 2)
+    z = me // IN_PLANE
+
+    def index(zz, yy, xx, cc):
+        return ((zz * 2 + yy) * 2 + xx) * 2 + cc
+
+    def block(zz, yy, xx, cc):
+        return pl.ds(pl.multiple_of(index(zz, yy, xx, cc) * rows, 16), rows)
+
+    to_x = (tm, index(z, py, 1 - px, core))
+    to_y = (tm, index(z, 1 - py, px, core))
+    to_c = (tm, index(z, py, px, 1 - core))
+    to_z = [None] + [(tm, index(lax.rem(z + d, PLANES), py, px, core)) for d in (1, 2, 3)]
+
+    loads = [
+        pltpu.make_async_copy(src, dst, load_sem.at[i])
+        for i, (src, dst) in enumerate([(w_hbm, w), (x_hbm, x), (cot_hbm, cot)])
+    ]
+    for c in loads:
+        c.start()
+
+    barrier = pltpu.get_barrier_semaphore()
+    for dev in (to_x, to_y, to_c, *to_z[1:]):
+        pl.semaphore_signal(barrier, inc=1, device_id=dev, device_id_type=MESH)
+
+    loads[0].wait()
+    own = block(z, py, px, core)
+    wide[own, :] = w[...].astype(BF16)
+
+    tap = taps_ref[1]
+    row = lax.broadcasted_iota(jnp.int32, (time_n, time_n), 0)
+    column = lax.broadcasted_iota(jnp.int32, (time_n, time_n), 1)
+    back = jnp.where(column == row - tap, 1.0, 0.0).astype(BF16)
+    ahead = jnp.where(column == row + tap, 1.0, 0.0).astype(BF16)
+    taps_at = [pl.ds(k * width, width) for k in range(3)]
+
+    def shift(s):
+        first = s * time_n
+        at = pl.ds(first, time_n)
+        xs[at, taps_at[0]] = x[s]
+        xs[at, taps_at[1]] = matmul(back, x[s]).astype(BF16)
+        xs[pl.ds(first, span), taps_at[2]] = jnp.zeros((span, width), BF16)
+        xs[pl.ds(first + span, time_n - span), taps_at[2]] = x[s, pl.ds(0, time_n - span), :]
+
+    def transpose(s):
+        first = s * time_n
+        at = pl.ds(first, time_n)
+        turned = x[s].T
+        xt[taps_at[0], at] = turned
+        xt[taps_at[1], at] = matmul(turned, ahead).astype(BF16)
+        xt[taps_at[2], pl.ds(first, span)] = jnp.zeros((width, span), BF16)
+        xt[taps_at[2], pl.ds(first + span, time_n - span)] = turned[:, : time_n - span]
+
+    loads[1].wait()
+    shift(0)
+    pl.semaphore_wait(barrier, 6)
+
+    def start(src, dst, sems, k, dev):
+        c = pltpu.make_async_remote_copy(
+            src_ref=src, dst_ref=dst, send_sem=sems[0].at[k], recv_sem=sems[1].at[k],
+            device_id=dev, device_id_type=MESH,
+        )
+        c.start()
+        return c
+
+    ag = (ag_send, ag_recv)
+    rs = (rs_send, rs_recv)
+    A, B, ALL = pl.ds(0, half), pl.ds(half, half), pl.ds(0, width)
+
+    def pass_on(blk, cols, k, dev):
+        return start(wide.at[blk, cols], wide.at[blk, cols], ag, k, dev)
+
+    def before(j):
+        return lax.rem(z + PLANES - j, PLANES)
+
+    z_in = [None] + [pass_on(own, ALL, d, to_z[d]) for d in (1, 2, 3)]
+    x1, y1, x2, y2, c_in = [], [], [], [], [[], [], [], []]
+
+    def first_hop(j):
+        if j:
+            z_in[j].wait_recv()
+        blk = block(before(j), py, px, core)
+        x1.append(pass_on(blk, ALL, 4 + j, to_x))
+        y1.append(pass_on(blk, ALL, 8 + j, to_y))
+        c_in[j].append(pass_on(blk, ALL, 12 + j, to_c))
+
+    def second_hop(j):
+        x1[j].wait_recv()
+        blk = block(before(j), py, 1 - px, core)
+        y2.append(pass_on(blk, A, 16 + j, to_y))
+        c_in[j].append(pass_on(blk, ALL, 20 + j, to_c))
+        y1[j].wait_recv()
+        blk = block(before(j), 1 - py, px, core)
+        x2.append(pass_on(blk, B, 24 + j, to_x))
+        c_in[j].append(pass_on(blk, ALL, 28 + j, to_c))
+
+    def last_hop(j):
+        y2[j].wait_recv()
+        x2[j].wait_recv()
+        c_in[j].append(pass_on(block(before(j), 1 - py, 1 - px, core), ALL, 32 + j, to_c))
+
+    def forward(j):
+        for c in c_in[j]:
+            c.wait_recv()
+        at = pl.ds(pl.multiple_of(before(j) * group, 128), group)
+        term = matmul(xs[:, at], wide[at, :])
+        pre[...] = term if j == 0 else pre[...] + term
+
+    first_hop(0)
+    shift(1)
+    first_hop(1)
+    second_hop(0)
+    transpose(0)
+    first_hop(2)
+    second_hop(1)
+    last_hop(0)
+    transpose(1)
+    first_hop(3)
+    second_hop(2)
+    last_hop(1)
+    forward(0)
+    second_hop(3)
+    last_hop(2)
+    forward(1)
+    last_hop(3)
+    forward(2)
+    loads[2].wait()
+    for c in c_in[3]:
+        c.wait_recv()
+    at = pl.ds(pl.multiple_of(before(3) * group, 128), group)
+    for s in range(series_n):
+        part = pl.ds(s * time_n, time_n)
+        total = pre[part, :] + matmul(xs[part, at], wide[at, :])
+        sig = jax.nn.sigmoid(total)
+        dk[0, part, :] = (cot[s].astype(F32) * (sig * (1.0 + total * (1.0 - sig)))).astype(BF16)
+
+    c1, a2, b2, a3, b3, z4 = {}, {}, {}, {}, {}, {}
+
+    def after(d):
+        return lax.rem(z + d, PLANES)
+
+    def weight_grad(d):
+        zz = after(d)
+        at = pl.ds(pl.multiple_of(zz * group, 128), group)
+        g[at, :] = matmul(xt[at, :], dk[0])
+        for q in range(4):
+            s1[d, q] = g[block(zz, q // 2, q % 2, 1 - core), :].astype(BF16)
+        c1[d] = start(s1.at[d], r1.at[d], rs, d, to_c)
+
+    def both(d, yy, xx, cols):
+        return g[block(after(d), yy, xx, core), cols] + r1[d, yy * 2 + xx, :, cols].astype(F32)
+
+    def reduce_one(d):
+        c1[d].wait_recv()
+        for q in range(2):
+            s2a[d, q] = both(d, q, 1 - px, A).astype(BF16)
+            s2b[d, q] = both(d, 1 - py, q, B).astype(BF16)
+        a2[d] = start(s2a.at[d], r2a.at[d], rs, 4 + d, to_x)
+        b2[d] = start(s2b.at[d], r2b.at[d], rs, 8 + d, to_y)
+
+    def reduce_two(d):
+        a2[d].wait_recv()
+        s3a[d] = (both(d, 1 - py, px, A) + r2a[d, 1 - py].astype(F32)).astype(BF16)
+        a3[d] = start(s3a.at[d], r3a.at[d], rs, 12 + d, to_y)
+        b2[d].wait_recv()
+        s3b[d] = (both(d, py, 1 - px, B) + r2b[d, 1 - px].astype(F32)).astype(BF16)
+        b3[d] = start(s3b.at[d], r3b.at[d], rs, 16 + d, to_x)
+
+    def reduce_three(d):
+        a3[d].wait_recv()
+        b3[d].wait_recv()
+        sum_a = both(d, py, px, A) + r2a[d, py].astype(F32) + r3a[d].astype(F32)
+        sum_b = both(d, py, px, B) + r2b[d, px].astype(F32) + r3b[d].astype(F32)
+        if d:
+            s4[d - 1, :, A] = sum_a.astype(BF16)
+            s4[d - 1, :, B] = sum_b.astype(BF16)
+            z4[d] = start(s4.at[d - 1], r4.at[d - 1], rs, 19 + d, to_z[d])
+        else:
+            grad_ref[:, A] = sum_a
+            grad_ref[:, B] = sum_b
+
+    stores = []
+
+    def shift_dpre(s):
+        first = s * time_n
+        dk[1, pl.ds(first, time_n), :] = matmul(ahead, dk[0, pl.ds(first, time_n), :]).astype(BF16)
+        dk[2, pl.ds(first, time_n - span), :] = dk[0, pl.ds(first + span, time_n - span), :]
+        dk[2, pl.ds(first + time_n - span, span), :] = jnp.zeros((span, width), BF16)
+
+    def grad_input(s):
+        total = cot[s].astype(F32)
+        for k in range(3):
+            total = total + matmul_t(dk[k, pl.ds(s * time_n, time_n), :], wide[taps_at[k], :])
+        gi[s] = total.astype(BF16)
+        c = pltpu.make_async_copy(gi.at[s], gi_hbm.at[s], store_sem.at[s])
+        c.start()
+        stores.append(c)
+
+    o = (2, 1, 3, 0)
+    weight_grad(o[0])
+    weight_grad(o[1])
+    reduce_one(o[0])
+    weight_grad(o[2])
+    reduce_one(o[1])
+    weight_grad(o[3])
+    reduce_one(o[2])
+    shift_dpre(0)
+    reduce_one(o[3])
+    reduce_two(o[0])
+    shift_dpre(1)
+    reduce_two(o[1])
+    grad_input(0)
+    reduce_two(o[2])
+    reduce_three(o[0])
+    reduce_two(o[3])
+    reduce_three(o[1])
+    grad_input(1)
+    reduce_three(o[2])
+    reduce_three(o[3])
+    total = grad_ref[...]
+    for d in (2, 1, 3):
+        z4[d].wait_recv()
+        total = total + r4[d - 1].astype(F32)
+    grad_ref[...] = total
+    c = pltpu.make_async_copy(grad_ref, grad_hbm, store_sem.at[series_n])
+    c.start()
+    stores.append(c)
+    for c in z_in[1:] + x1 + y1 + x2 + y2 + sum(c_in, []):
+        c.wait_send()
+    for made in (c1, a2, b2, a3, b3, z4):
+        for c in made.values():
+            c.wait_send()
+    for c in stores:
+        c.wait()
+
+
+def finish(gi, grad, weight, moment_one, second_moment_state, gi_out, nw, n1, n2, sems):
+    copies = [pltpu.make_async_copy(gi.at[s], gi_out.at[s], sems.at[s]) for s in range(gi.shape[0])]
+    for c in copies:
+        c.start()
+    nw[...], n1[...], n2[...] = adamw(weight[...], grad[...], moment_one[...], second_moment_state[...])
+    for c in copies:
+        c.wait()
+
+
+def fused(inputs, cotangent, taps, weight, moment_one, second_moment_state):
+    series_n, time_n, width = inputs.shape
+    rows = weight.shape[0]
+    depth = taps.shape[0] * width
+    half = width // 2
+    flat = series_n * time_n
+    state = jax.ShapeDtypeStruct(weight.shape, F32)
+    hbm = pl.BlockSpec(memory_space=pltpu.HBM)
+    vmem = pl.BlockSpec(memory_space=pltpu.VMEM)
+    V = pltpu.VMEM
+    gi, grad = pl.pallas_call(
+        kernel,
+        out_shape=[jax.ShapeDtypeStruct(inputs.shape, BF16), state],
+        in_specs=[pl.BlockSpec(memory_space=pltpu.SMEM)] + [hbm] * 3,
+        out_specs=[hbm] * 2,
+        scratch_shapes=[
+            V(inputs.shape, BF16), V(inputs.shape, BF16), V(weight.shape, F32),
+            V(inputs.shape, BF16), V(weight.shape, F32),
+            V((depth, width), BF16),
+            V((flat, depth), BF16),
+            V((depth, flat), BF16),
+            V((flat, width), F32),
+            V((3, flat, width), BF16),
+            V((depth, width), F32),
+            V((PLANES, 4, rows, width), BF16), V((PLANES, 4, rows, width), BF16),
+            V((PLANES, 2, rows, half), BF16), V((PLANES, 2, rows, half), BF16),
+            V((PLANES, 2, rows, half), BF16), V((PLANES, 2, rows, half), BF16),
+            V((PLANES, rows, half), BF16), V((PLANES, rows, half), BF16),
+            V((PLANES, rows, half), BF16), V((PLANES, rows, half), BF16),
+            V((3, rows, width), BF16), V((3, rows, width), BF16),
+            pltpu.SemaphoreType.DMA((3,)), pltpu.SemaphoreType.DMA((series_n + 1,)),
+            pltpu.SemaphoreType.DMA((36,)), pltpu.SemaphoreType.DMA((36,)),
+            pltpu.SemaphoreType.DMA((23,)), pltpu.SemaphoreType.DMA((23,)),
+        ],
+        compiler_params=pltpu.CompilerParams(
+            collective_id=0, has_side_effects=True, vmem_limit_bytes=63 * 1024 * 1024
+        ),
+        cost_estimate=pl.CostEstimate(
+            flops=6 * flat * depth * width, bytes_accessed=6 * flat * width, transcendentals=flat * width
+        ),
+    )(taps, inputs, cotangent, weight)
+    return tuple(pl.pallas_call(
+        finish,
+        out_shape=[jax.ShapeDtypeStruct(inputs.shape, BF16), state, state, state],
+        in_specs=[hbm] + [vmem] * 4,
+        out_specs=[hbm] + [vmem] * 3,
+        scratch_shapes=[pltpu.SemaphoreType.DMA((series_n,))],
+        compiler_params=pltpu.CompilerParams(vmem_limit_bytes=65024 * 1024),
+        cost_estimate=pl.CostEstimate(flops=20 * rows * width, bytes_accessed=28 * rows * width, transcendentals=0),
+    )(gi, grad, weight, moment_one, second_moment_state))
+
+
 def solution(mesh):
     in_specs = (
         P("series", "tm", None),
@@ -78,4 +412,5 @@
         P("series", None),
     )
     out_specs = (P("series", "tm", None), P("series", None), P("series", None), P("series", None))
-    return jax.shard_map(body, mesh=mesh, in_specs=in_specs, out_specs=out_specs, check_vma=False)
+    step = fused if fits(mesh) else body
+    return jax.shard_map(step, mesh=mesh, in_specs=in_specs, out_specs=out_specs, check_vma=False)

time: 187 us -> 74 us (0.40)
  waiting for transfers between devices: 137 us -> 0 us
  Pallas kernels: 0 us -> 73.2 us
  between operations: 23.8 us -> 0.64 us
  matrix products: 10.8 us -> 0 us
  local copies, waits for them, and re-layouts: 7.16 us -> 0 us
  other arithmetic: 6.47 us -> 0 us
    reduce_scatter x1 -> x0, waiting for transfers between devices: 86 us -> none  [body(): lax.psum_scatter(lax.dot_general(stacked, dpre_flat, (((0,), (0,)), ((),...]
    pallas_call x0 -> x2, Pallas kernels: none -> 73.2 us  [the longest x1 38.6 us: fused(): pl.pallas_call(kernel, out_shape=[jax.ShapeDtypeStruct(inputs.shape, BF16...]
    all_gather x1 -> x0, waiting for transfers between devices: 51 us -> none  [body(): lax.all_gather(weight.astype(jnp.bfloat16), 'series', axis=0, tiled=True)]
    dot_general x5 -> x0, matrix products: 10.8 us -> none  [the longest x1 4.04 us: body(): pre = jnp.dot(stacked, wide, preferred_element_type=jnp.float32)]
    concatenate x2 -> x0, other arithmetic: 3.31 us -> none  [the longest x1 3.05 us: body(): later = jnp.concatenate([dpre, ahead], 1)]
    unnamed x15 -> x0, local copies, waits for them, and re-layouts: 2.69 us -> none
    slice x3 -> x0, local copies, waits for them, and re-layouts: 2.37 us -> none  [the longest x1 1.38 us: body(): taps[k]]
  transfers between devices with their start and end apart: 4 -> 0, of which waited for: 2 -> 0; matrix products, arithmetic and copies ran while one was open for 6% -> 0% of each run, Pallas kernels for 0% -> 0%
where the time goes in v2:
time: 74 us; the launch traced here: 73.8 us
  Pallas kernels  73.2 us (99%)
    pallas_call x1, Pallas kernels, fused(): pl.pallas_call(kernel, out_shape=[jax.ShapeDtypeStruct(inputs.shape, BF16...  38.6 us
    pallas_call x1, Pallas kernels, fused(): pl.pallas_call(finish, out_shape=[jax.ShapeDtypeStruct(inputs.shape, BF16...  34.6 us

profile of v2, /device:TPU:0, one launch (start us, length us, event | category | flops | bytes accessed | tf_op | source)
XLA Modules:
  0.0 73.8 jit_solution(5213726842880137000)
XLA Ops:
  0.6 38.6 %shard_map.93 = (bf16[2,512,512]{2,1,0:T(8,128)(2,1)}, f32[48,512]{1,0:T(8,128)}) custom-call(s32[3]{0:T(128)} %taps_ref.1, bf16[2,512,512]{2,1,0:T(8,128)(2,1)} %x_hbm.1, bf16[2,512,512]{2,1,0:T(8,128)(2,1)} %cot_hbm.1, f32[48,512]{1,0:T(8,128)} %weight.1), custom_call_target="tpu_custom_call" | custom-call | flops 4831838208 | bytes 3145728 | tf_op jit(solution)/shard_map/pallas_call | solution.py:363
  39.2 34.6 %shard_map.94 = (bf16[2,512,512]{2,1,0:T(8,128)(2,1)}, f32[48,512]{1,0:T(8,128)}, f32[48,512]{1,0:T(8,128)}, f32[48,512]{1,0:T(8,128)}) custom-call(bf16[2,512,512]{2,1,0:T(8,128)(2,1)} %get-tuple-element.6.gi, f32[48,512]{1,0:T(8,128)} %get-tuple-element.7.grad, f32[48,512]{1,0:T(8,128)} %weight.1, f32[48,512]{1,0:T(8,128)} %moment_one.1, ...), custom_call_target="tpu_custom_call" | custom-call | flops 491520 | bytes 688128 | tf_op jit(solution)/shard_map/pallas_call | solution.py:394

commit v3 on v2

--- a/solution.py
+++ b/solution.py
@@ -341,12 +341,30 @@
         c.wait()
 
 
-def finish(gi, grad, weight, moment_one, second_moment_state, gi_out, nw, n1, n2, sems):
-    copies = [pltpu.make_async_copy(gi.at[s], gi_out.at[s], sems.at[s]) for s in range(gi.shape[0])]
-    for c in copies:
+def finish(
+    gi, grad, weight, moment_one, second_moment_state, gi_out, nw_out, n1_out, n2_out,
+    held, state, new, in_sem, out_sem, state_sem, new_sem,
+):
+    parts = [(s, pl.ds(h * held.shape[1] // 2, held.shape[1] // 2)) for s in range(held.shape[0]) for h in range(2)]
+    inward = [pltpu.make_async_copy(gi.at[p], held.at[p], in_sem.at[i]) for i, p in enumerate(parts)]
+    states = [
+        pltpu.make_async_copy(src, state.at[i], state_sem.at[i])
+        for i, src in enumerate((weight, grad, moment_one, second_moment_state))
+    ]
+    for c in inward + states:
         c.start()
-    nw[...], n1[...], n2[...] = adamw(weight[...], grad[...], moment_one[...], second_moment_state[...])
-    for c in copies:
+    outward = []
+    for i, p in enumerate(parts):
+        inward[i].wait()
+        outward.append(pltpu.make_async_copy(held.at[p], gi_out.at[p], out_sem.at[i]))
+        outward[-1].start()
+    for c in states:
+        c.wait()
+    new[0], new[1], new[2] = adamw(state[0], state[1], state[2], state[3])
+    for i, dst in enumerate((nw_out, n1_out, n2_out)):
+        outward.append(pltpu.make_async_copy(new.at[i], dst, new_sem.at[i]))
+        outward[-1].start()
+    for c in outward:
         c.wait()
 
 
@@ -358,7 +376,6 @@
     flat = series_n * time_n
     state = jax.ShapeDtypeStruct(weight.shape, F32)
     hbm = pl.BlockSpec(memory_space=pltpu.HBM)
-    vmem = pl.BlockSpec(memory_space=pltpu.VMEM)
     V = pltpu.VMEM
     gi, grad = pl.pallas_call(
         kernel,
@@ -394,10 +411,14 @@
     return tuple(pl.pallas_call(
         finish,
         out_shape=[jax.ShapeDtypeStruct(inputs.shape, BF16), state, state, state],
-        in_specs=[hbm] + [vmem] * 4,
-        out_specs=[hbm] + [vmem] * 3,
-        scratch_shapes=[pltpu.SemaphoreType.DMA((series_n,))],
-        compiler_params=pltpu.CompilerParams(vmem_limit_bytes=65024 * 1024),
+        in_specs=[hbm] * 5,
+        out_specs=[hbm] * 4,
+        scratch_shapes=[
+            V(inputs.shape, BF16), V((4, rows, width), F32), V((3, rows, width), F32),
+            pltpu.SemaphoreType.DMA((2 * series_n,)), pltpu.SemaphoreType.DMA((2 * series_n,)),
+            pltpu.SemaphoreType.DMA((4,)), pltpu.SemaphoreType.DMA((3,)),
+        ],
+        compiler_params=pltpu.CompilerParams(vmem_limit_bytes=63 * 1024 * 1024),
         cost_estimate=pl.CostEstimate(flops=20 * rows * width, bytes_accessed=28 * rows * width, transcendentals=0),
     )(gi, grad, weight, moment_one, second_moment_state))
 

time: 74 us -> 41.6 us (0.56)
  Pallas kernels: 73.2 us -> 40.8 us
    pallas_call x1, Pallas kernels: 34.6 us -> 2.24 us  [fused(): pl.pallas_call(finish, out_shape=[jax.ShapeDtypeStruct(inputs.shape, BF16...]
where the time goes in v3:
time: 41.6 us; the launch traced here: 41.5 us
  Pallas kernels  40.8 us (98%)
  between operations  0.64 us (2%)
    pallas_call x1, Pallas kernels, fused(): pl.pallas_call(kernel, out_shape=[jax.ShapeDtypeStruct(inputs.shape, BF16...  38.6 us
    pallas_call x1, Pallas kernels, fused(): pl.pallas_call(finish, out_shape=[jax.ShapeDtypeStruct(inputs.shape, BF16...  2.24 us

profile of v3, /device:TPU:0, one launch (start us, length us, event | category | flops | bytes accessed | tf_op | source)
XLA Modules:
  0.0 41.5 jit_solution(949214676720365820)
XLA Ops:
  0.6 38.6 %shard_map.93 = (bf16[2,512,512]{2,1,0:T(8,128)(2,1)}, f32[48,512]{1,0:T(8,128)}) custom-call(s32[3]{0:T(128)} %taps_ref.1, bf16[2,512,512]{2,1,0:T(8,128)(2,1)} %x_hbm.1, bf16[2,512,512]{2,1,0:T(8,128)(2,1)} %cot_hbm.1, f32[48,512]{1,0:T(8,128)} %weight.1), custom_call_target="tpu_custom_call" | custom-call | flops 4831838208 | bytes 3145728 | tf_op jit(solution)/shard_map/pallas_call | solution.py:380
  39.2 2.2 %shard_map.94 = (bf16[2,512,512]{2,1,0:T(8,128)(2,1)}, f32[48,512]{1,0:T(8,128)}, f32[48,512]{1,0:T(8,128)}, f32[48,512]{1,0:T(8,128)}) custom-call(bf16[2,512,512]{2,1,0:T(8,128)(2,1)} %get-tuple-element.6.gi, f32[48,512]{1,0:T(8,128)} %get-tuple-element.7.grad, f32[48,512]{1,0:T(8,128)} %weight.1, f32[48,512]{1,0:T(8,128)} %moment_one.1, ...), custom_call_target="tpu_custom_call" | custom-call | flops 491520 | bytes 688128 | tf_op jit(solution)/shard_map/pallas_call | solution.py:411

commit v4 on v3

--- a/solution.py
+++ b/solution.py
@@ -134,32 +134,6 @@
     own = block(z, py, px, core)
     wide[own, :] = w[...].astype(BF16)
 
-    tap = taps_ref[1]
-    row = lax.broadcasted_iota(jnp.int32, (time_n, time_n), 0)
-    column = lax.broadcasted_iota(jnp.int32, (time_n, time_n), 1)
-    back = jnp.where(column == row - tap, 1.0, 0.0).astype(BF16)
-    ahead = jnp.where(column == row + tap, 1.0, 0.0).astype(BF16)
-    taps_at = [pl.ds(k * width, width) for k in range(3)]
-
-    def shift(s):
-        first = s * time_n
-        at = pl.ds(first, time_n)
-        xs[at, taps_at[0]] = x[s]
-        xs[at, taps_at[1]] = matmul(back, x[s]).astype(BF16)
-        xs[pl.ds(first, span), taps_at[2]] = jnp.zeros((span, width), BF16)
-        xs[pl.ds(first + span, time_n - span), taps_at[2]] = x[s, pl.ds(0, time_n - span), :]
-
-    def transpose(s):
-        first = s * time_n
-        at = pl.ds(first, time_n)
-        turned = x[s].T
-        xt[taps_at[0], at] = turned
-        xt[taps_at[1], at] = matmul(turned, ahead).astype(BF16)
-        xt[taps_at[2], pl.ds(first, span)] = jnp.zeros((width, span), BF16)
-        xt[taps_at[2], pl.ds(first + span, time_n - span)] = turned[:, : time_n - span]
-
-    loads[1].wait()
-    shift(0)
     pl.semaphore_wait(barrier, 6)
 
     def start(src, dst, sems, k, dev):
@@ -214,32 +188,66 @@
         pre[...] = term if j == 0 else pre[...] + term
 
     first_hop(0)
-    shift(1)
+    tap = taps_ref[1]
+    row = lax.broadcasted_iota(jnp.int32, (time_n, time_n), 0)
+    column = lax.broadcasted_iota(jnp.int32, (time_n, time_n), 1)
+    back = jnp.where(column == row - tap, 1.0, 0.0).astype(BF16)
+    ahead = jnp.where(column == row + tap, 1.0, 0.0).astype(BF16)
+    taps_at = [pl.ds(k * width, width) for k in range(3)]
+
+    def shift(s):
+        first = s * time_n
+        at = pl.ds(first, time_n)
+        xs[at, taps_at[0]] = x[s]
+        xs[at, taps_at[1]] = matmul(back, x[s]).astype(BF16)
+        xs[pl.ds(first, span), taps_at[2]] = jnp.zeros((span, width), BF16)
+        xs[pl.ds(first + span, time_n - span), taps_at[2]] = x[s, pl.ds(0, time_n - span), :]
+
+    def transpose(s, h):
+        first = s * time_n
+        at = pl.ds(first, time_n)
+        turned = x[s, :, pl.ds(h * half, half)].T
+        xt[pl.ds(h * half, half), at] = turned
+        xt[pl.ds(width + h * half, half), at] = matmul(turned, ahead).astype(BF16)
+        last = pl.ds(2 * width + h * half, half)
+        xt[last, pl.ds(first, span)] = jnp.zeros((half, span), BF16)
+        xt[last, pl.ds(first + span, time_n - span)] = turned[:, : time_n - span]
+
+    loads[1].wait()
+    shift(0)
     first_hop(1)
     second_hop(0)
-    transpose(0)
+    shift(1)
     first_hop(2)
     second_hop(1)
     last_hop(0)
-    transpose(1)
+    transpose(0, 0)
     first_hop(3)
     second_hop(2)
     last_hop(1)
-    forward(0)
+    transpose(0, 1)
     second_hop(3)
     last_hop(2)
+    forward(0)
+    last_hop(3)
+    transpose(1, 0)
+    transpose(1, 1)
     forward(1)
-    last_hop(3)
     forward(2)
     loads[2].wait()
     for c in c_in[3]:
         c.wait_recv()
     at = pl.ds(pl.multiple_of(before(3) * group, 128), group)
-    for s in range(series_n):
-        part = pl.ds(s * time_n, time_n)
+    step = 256
+    fine = 32
+    for first in range(0, flat, step):
+        part = pl.ds(first, step)
         total = pre[part, :] + matmul(xs[part, at], wide[at, :])
-        sig = jax.nn.sigmoid(total)
-        dk[0, part, :] = (cot[s].astype(F32) * (sig * (1.0 + total * (1.0 - sig)))).astype(BF16)
+        for f in range(0, step, fine):
+            t = total[f : f + fine]
+            sig = 0.5 * jnp.tanh(0.5 * t) + 0.5
+            up = cot[first // time_n, pl.ds(first % time_n + f, fine), :].astype(F32)
+            dk[0, pl.ds(first + f, fine), :] = (up * (sig * (1.0 + t * (1.0 - sig)))).astype(BF16)
 
     c1, a2, b2, a3, b3, z4 = {}, {}, {}, {}, {}, {}
 
@@ -294,12 +302,15 @@
         dk[2, pl.ds(first, time_n - span), :] = dk[0, pl.ds(first + span, time_n - span), :]
         dk[2, pl.ds(first + time_n - span, span), :] = jnp.zeros((span, width), BF16)
 
-    def grad_input(s):
-        total = cot[s].astype(F32)
+    def grad_input(i):
+        size = time_n // 2
+        s, first = i // 2, (i % 2) * size
+        total = cot[s, pl.ds(first, size), :].astype(F32)
         for k in range(3):
-            total = total + matmul_t(dk[k, pl.ds(s * time_n, time_n), :], wide[taps_at[k], :])
-        gi[s] = total.astype(BF16)
-        c = pltpu.make_async_copy(gi.at[s], gi_hbm.at[s], store_sem.at[s])
+            total = total + matmul_t(dk[k, pl.ds(i * size, size), :], wide[taps_at[k], :])
+        gi[s, pl.ds(first, size), :] = total.astype(BF16)
+        part = (s, pl.ds(first, size))
+        c = pltpu.make_async_copy(gi.at[part], gi_hbm.at[part], store_sem.at[i])
         c.start()
         stores.append(c)
 
@@ -314,22 +325,24 @@
     shift_dpre(0)
     reduce_one(o[3])
     reduce_two(o[0])
+    grad_input(0)
+    reduce_two(o[1])
+    reduce_three(o[0])
+    grad_input(1)
+    reduce_two(o[2])
+    reduce_three(o[1])
     shift_dpre(1)
-    reduce_two(o[1])
-    grad_input(0)
-    reduce_two(o[2])
-    reduce_three(o[0])
     reduce_two(o[3])
-    reduce_three(o[1])
-    grad_input(1)
     reduce_three(o[2])
+    grad_input(2)
     reduce_three(o[3])
+    grad_input(3)
     total = grad_ref[...]
     for d in (2, 1, 3):
         z4[d].wait_recv()
         total = total + r4[d - 1].astype(F32)
     grad_ref[...] = total
-    c = pltpu.make_async_copy(grad_ref, grad_hbm, store_sem.at[series_n])
+    c = pltpu.make_async_copy(grad_ref, grad_hbm, store_sem.at[2 * series_n])
     c.start()
     stores.append(c)
     for c in z_in[1:] + x1 + y1 + x2 + y2 + sum(c_in, []):
@@ -397,7 +410,7 @@
             V((PLANES, rows, half), BF16), V((PLANES, rows, half), BF16),
             V((PLANES, rows, half), BF16), V((PLANES, rows, half), BF16),
             V((3, rows, width), BF16), V((3, rows, width), BF16),
-            pltpu.SemaphoreType.DMA((3,)), pltpu.SemaphoreType.DMA((series_n + 1,)),
+            pltpu.SemaphoreType.DMA((3,)), pltpu.SemaphoreType.DMA((2 * series_n + 1,)),
             pltpu.SemaphoreType.DMA((36,)), pltpu.SemaphoreType.DMA((36,)),
             pltpu.SemaphoreType.DMA((23,)), pltpu.SemaphoreType.DMA((23,)),
         ],

time: 41.6 us -> 42.5 us (1.022)
  Pallas kernels: 40.8 us -> 41.7 us
    pallas_call x1, Pallas kernels: 38.6 us -> 39.4 us  [fused(): pl.pallas_call(kernel, out_shape=[jax.ShapeDtypeStruct(inputs.shape, BF16...]
where the time goes in v4:
time: 42.5 us; the launch traced here: 42.3 us
  Pallas kernels  41.7 us (98%)
  between operations  0.64 us (2%)
    pallas_call x1, Pallas kernels, fused(): pl.pallas_call(kernel, out_shape=[jax.ShapeDtypeStruct(inputs.shape, BF16...  39.4 us
    pallas_call x1, Pallas kernels, fused(): pl.pallas_call(finish, out_shape=[jax.ShapeDtypeStruct(inputs.shape, BF16...  2.24 us

profile of v4, /device:TPU:0, one launch (start us, length us, event | category | flops | bytes accessed | tf_op | source)
XLA Modules:
  0.0 42.3 jit_solution(9455212226003180466)
XLA Ops:
  0.6 39.4 %shard_map.93 = (bf16[2,512,512]{2,1,0:T(8,128)(2,1)}, f32[48,512]{1,0:T(8,128)}) custom-call(s32[3]{0:T(128)} %taps_ref.1, bf16[2,512,512]{2,1,0:T(8,128)(2,1)} %x_hbm.1, bf16[2,512,512]{2,1,0:T(8,128)(2,1)} %cot_hbm.1, f32[48,512]{1,0:T(8,128)} %weight.1), custom_call_target="tpu_custom_call" | custom-call | flops 4831838208 | bytes 3145728 | tf_op jit(solution)/shard_map/pallas_call | solution.py:393
  40.1 2.2 %shard_map.94 = (bf16[2,512,512]{2,1,0:T(8,128)(2,1)}, f32[48,512]{1,0:T(8,128)}, f32[48,512]{1,0:T(8,128)}, f32[48,512]{1,0:T(8,128)}) custom-call(bf16[2,512,512]{2,1,0:T(8,128)(2,1)} %get-tuple-element.6.gi, f32[48,512]{1,0:T(8,128)} %get-tuple-element.7.grad, f32[48,512]{1,0:T(8,128)} %weight.1, f32[48,512]{1,0:T(8,128)} %moment_one.1, ...), custom_call_target="tpu_custom_call" | custom-call | flops 491520 | bytes 688128 | tf_op jit(solution)/shard_map/pallas_call | solution.py:424

commit v5 on v4

--- a/solution.py
+++ b/solution.py
@@ -92,7 +92,7 @@
 def kernel(
     taps_ref, x_hbm, cot_hbm, w_hbm, gi_hbm, grad_hbm,
     x, cot, w, gi, grad_ref,
-    wide, xs, xt, pre, dk, g, s1, r1, s2a, s2b, r2a, r2b, s3a, s3b, r3a, r3b, s4, r4,
+    wide, xs, xt, pre, dk, g, s1, r1, s2, r2, s3, r3,
     load_sem, store_sem, ag_send, ag_recv, rs_send, rs_recv,
 ):
     series_n, time_n, width = x.shape
@@ -116,6 +116,7 @@
 
     to_x = (tm, index(z, py, 1 - px, core))
     to_y = (tm, index(z, 1 - py, px, core))
+    to_d = (tm, index(z, 1 - py, 1 - px, core))
     to_c = (tm, index(z, py, px, 1 - core))
     to_z = [None] + [(tm, index(lax.rem(z + d, PLANES), py, px, core)) for d in (1, 2, 3)]
 
@@ -123,18 +124,17 @@
         pltpu.make_async_copy(src, dst, load_sem.at[i])
         for i, (src, dst) in enumerate([(w_hbm, w), (x_hbm, x), (cot_hbm, cot)])
     ]
-    for c in loads:
-        c.start()
+    loads[0].start()
 
     barrier = pltpu.get_barrier_semaphore()
-    for dev in (to_x, to_y, to_c, *to_z[1:]):
+    for dev in (to_x, to_y, to_d, to_c, *to_z[1:]):
         pl.semaphore_signal(barrier, inc=1, device_id=dev, device_id_type=MESH)
 
     loads[0].wait()
     own = block(z, py, px, core)
     wide[own, :] = w[...].astype(BF16)
 
-    pl.semaphore_wait(barrier, 6)
+    pl.semaphore_wait(barrier, 7)
 
     def start(src, dst, sems, k, dev):
         c = pltpu.make_async_remote_copy(
@@ -146,39 +146,28 @@
 
     ag = (ag_send, ag_recv)
     rs = (rs_send, rs_recv)
-    A, B, ALL = pl.ds(0, half), pl.ds(half, half), pl.ds(0, width)
-
-    def pass_on(blk, cols, k, dev):
-        return start(wide.at[blk, cols], wide.at[blk, cols], ag, k, dev)
+
+    def pass_on(blk, k, dev):
+        return start(wide.at[blk, :], wide.at[blk, :], ag, k, dev)
 
     def before(j):
         return lax.rem(z + PLANES - j, PLANES)
 
-    z_in = [None] + [pass_on(own, ALL, d, to_z[d]) for d in (1, 2, 3)]
-    x1, y1, x2, y2, c_in = [], [], [], [], [[], [], [], []]
+    z_in = [None] + [pass_on(own, d, to_z[d]) for d in (1, 2, 3)]
+    plane = [(to_x, py, 1 - px), (to_y, 1 - py, px), (to_d, 1 - py, 1 - px)]
+    p_in, c_in = [], [[], [], [], []]
 
     def first_hop(j):
         if j:
             z_in[j].wait_recv()
         blk = block(before(j), py, px, core)
-        x1.append(pass_on(blk, ALL, 4 + j, to_x))
-        y1.append(pass_on(blk, ALL, 8 + j, to_y))
-        c_in[j].append(pass_on(blk, ALL, 12 + j, to_c))
+        p_in.append([pass_on(blk, 4 + 4 * i + j, to) for i, (to, _, _) in enumerate(plane)])
+        c_in[j].append(pass_on(blk, 16 + j, to_c))
 
     def second_hop(j):
-        x1[j].wait_recv()
-        blk = block(before(j), py, 1 - px, core)
-        y2.append(pass_on(blk, A, 16 + j, to_y))
-        c_in[j].append(pass_on(blk, ALL, 20 + j, to_c))
-        y1[j].wait_recv()
-        blk = block(before(j), 1 - py, px, core)
-        x2.append(pass_on(blk, B, 24 + j, to_x))
-        c_in[j].append(pass_on(blk, ALL, 28 + j, to_c))
-
-    def last_hop(j):
-        y2[j].wait_recv()
-        x2[j].wait_recv()
-        c_in[j].append(pass_on(block(before(j), 1 - py, 1 - px, core), ALL, 32 + j, to_c))
+        for i, (_, yy, xx) in enumerate(plane):
+            p_in[j][i].wait_recv()
+            c_in[j].append(pass_on(block(before(j), yy, xx, core), 20 + 4 * i + j, to_c))
 
     def forward(j):
         for c in c_in[j]:
@@ -188,6 +177,7 @@
         pre[...] = term if j == 0 else pre[...] + term
 
     first_hop(0)
+    loads[1].start()
     tap = taps_ref[1]
     row = lax.broadcasted_iota(jnp.int32, (time_n, time_n), 0)
     column = lax.broadcasted_iota(jnp.int32, (time_n, time_n), 1)
@@ -213,23 +203,20 @@
         xt[last, pl.ds(first, span)] = jnp.zeros((half, span), BF16)
         xt[last, pl.ds(first + span, time_n - span)] = turned[:, : time_n - span]
 
+    first_hop(1)
     loads[1].wait()
+    loads[2].start()
     shift(0)
-    first_hop(1)
+    first_hop(2)
     second_hop(0)
     shift(1)
-    first_hop(2)
+    first_hop(3)
     second_hop(1)
-    last_hop(0)
     transpose(0, 0)
-    first_hop(3)
     second_hop(2)
-    last_hop(1)
+    forward(0)
     transpose(0, 1)
     second_hop(3)
-    last_hop(2)
-    forward(0)
-    last_hop(3)
     transpose(1, 0)
     transpose(1, 1)
     forward(1)
@@ -249,7 +236,7 @@
             up = cot[first // time_n, pl.ds(first % time_n + f, fine), :].astype(F32)
             dk[0, pl.ds(first + f, fine), :] = (up * (sig * (1.0 + t * (1.0 - sig)))).astype(BF16)
 
-    c1, a2, b2, a3, b3, z4 = {}, {}, {}, {}, {}, {}
+    c1, p2, z4 = {}, {}, {}
 
     def after(d):
         return lax.rem(z + d, PLANES)
@@ -262,37 +249,26 @@
             s1[d, q] = g[block(zz, q // 2, q % 2, 1 - core), :].astype(BF16)
         c1[d] = start(s1.at[d], r1.at[d], rs, d, to_c)
 
-    def both(d, yy, xx, cols):
-        return g[block(after(d), yy, xx, core), cols] + r1[d, yy * 2 + xx, :, cols].astype(F32)
+    def chip_sum(d, yy, xx):
+        return g[block(after(d), yy, xx, core), :] + r1[d, yy * 2 + xx].astype(F32)
 
     def reduce_one(d):
         c1[d].wait_recv()
-        for q in range(2):
-            s2a[d, q] = both(d, q, 1 - px, A).astype(BF16)
-            s2b[d, q] = both(d, 1 - py, q, B).astype(BF16)
-        a2[d] = start(s2a.at[d], r2a.at[d], rs, 4 + d, to_x)
-        b2[d] = start(s2b.at[d], r2b.at[d], rs, 8 + d, to_y)
+        p2[d] = []
+        for i, (to, yy, xx) in enumerate(plane):
+            s2[d, i] = chip_sum(d, yy, xx).astype(BF16)
+            p2[d].append(start(s2.at[d, i], r2.at[d, i], rs, 4 + 3 * d + i, to))
 
     def reduce_two(d):
-        a2[d].wait_recv()
-        s3a[d] = (both(d, 1 - py, px, A) + r2a[d, 1 - py].astype(F32)).astype(BF16)
-        a3[d] = start(s3a.at[d], r3a.at[d], rs, 12 + d, to_y)
-        b2[d].wait_recv()
-        s3b[d] = (both(d, py, 1 - px, B) + r2b[d, 1 - px].astype(F32)).astype(BF16)
-        b3[d] = start(s3b.at[d], r3b.at[d], rs, 16 + d, to_x)
-
-    def reduce_three(d):
-        a3[d].wait_recv()
-        b3[d].wait_recv()
-        sum_a = both(d, py, px, A) + r2a[d, py].astype(F32) + r3a[d].astype(F32)
-        sum_b = both(d, py, px, B) + r2b[d, px].astype(F32) + r3b[d].astype(F32)
+        total = chip_sum(d, py, px)
+        for i in range(3):
+            p2[d][i].wait_recv()
+            total = total + r2[d, i].astype(F32)
         if d:
-            s4[d - 1, :, A] = sum_a.astype(BF16)
-            s4[d - 1, :, B] = sum_b.astype(BF16)
-            z4[d] = start(s4.at[d - 1], r4.at[d - 1], rs, 19 + d, to_z[d])
+            s3[d - 1] = total.astype(BF16)
+            z4[d] = start(s3.at[d - 1], r3.at[d - 1], rs, 15 + d, to_z[d])
         else:
-            grad_ref[:, A] = sum_a
-            grad_ref[:, B] = sum_b
+            grad_ref[...] = total
 
     stores = []
 
@@ -322,32 +298,28 @@
     reduce_one(o[1])
     weight_grad(o[3])
     reduce_one(o[2])
+    reduce_one(o[3])
     shift_dpre(0)
-    reduce_one(o[3])
     reduce_two(o[0])
     grad_input(0)
     reduce_two(o[1])
-    reduce_three(o[0])
     grad_input(1)
     reduce_two(o[2])
-    reduce_three(o[1])
     shift_dpre(1)
     reduce_two(o[3])
-    reduce_three(o[2])
     grad_input(2)
-    reduce_three(o[3])
     grad_input(3)
     total = grad_ref[...]
     for d in (2, 1, 3):
         z4[d].wait_recv()
-        total = total + r4[d - 1].astype(F32)
+        total = total + r3[d - 1].astype(F32)
     grad_ref[...] = total
     c = pltpu.make_async_copy(grad_ref, grad_hbm, store_sem.at[2 * series_n])
     c.start()
     stores.append(c)
-    for c in z_in[1:] + x1 + y1 + x2 + y2 + sum(c_in, []):
+    for c in z_in[1:] + sum(p_in, []) + sum(c_in, []) + sum(p2.values(), []):
         c.wait_send()
-    for made in (c1, a2, b2, a3, b3, z4):
+    for made in (c1, z4):
         for c in made.values():
             c.wait_send()
     for c in stores:
@@ -385,7 +357,6 @@
     series_n, time_n, width = inputs.shape
     rows = weight.shape[0]
     depth = taps.shape[0] * width
-    half = width // 2
     flat = series_n * time_n
     state = jax.ShapeDtypeStruct(weight.shape, F32)
     hbm = pl.BlockSpec(memory_space=pltpu.HBM)
@@ -405,14 +376,11 @@
             V((3, flat, width), BF16),
             V((depth, width), F32),
             V((PLANES, 4, rows, width), BF16), V((PLANES, 4, rows, width), BF16),
-            V((PLANES, 2, rows, half), BF16), V((PLANES, 2, rows, half), BF16),
-            V((PLANES, 2, rows, half), BF16), V((PLANES, 2, rows, half), BF16),
-            V((PLANES, rows, half), BF16), V((PLANES, rows, half), BF16),
-            V((PLANES, rows, half), BF16), V((PLANES, rows, half), BF16),
+            V((PLANES, 3, rows, width), BF16), V((PLANES, 3, rows, width), BF16),
             V((3, rows, width), BF16), V((3, rows, width), BF16),
             pltpu.SemaphoreType.DMA((3,)), pltpu.SemaphoreType.DMA((2 * series_n + 1,)),
-            pltpu.SemaphoreType.DMA((36,)), pltpu.SemaphoreType.DMA((36,)),
-            pltpu.SemaphoreType.DMA((23,)), pltpu.SemaphoreType.DMA((23,)),
+            pltpu.SemaphoreType.DMA((32,)), pltpu.SemaphoreType.DMA((32,)),
+            pltpu.SemaphoreType.DMA((19,)), pltpu.SemaphoreType.DMA((19,)),
         ],
         compiler_params=pltpu.CompilerParams(
             collective_id=0, has_side_effects=True, vmem_limit_bytes=63 * 1024 * 1024

time: 42.5 us -> 38.4 us (0.904)
  Pallas kernels: 41.7 us -> 37.6 us
    pallas_call x1, Pallas kernels: 39.4 us -> 35.3 us  [fused(): pl.pallas_call(kernel, out_shape=[jax.ShapeDtypeStruct(inputs.shape, BF16...]
where the time goes in v5:
time: 38.4 us; the launch traced here: 38.2 us
  Pallas kernels  37.6 us (98%)
  between operations  0.64 us (2%)
    pallas_call x1, Pallas kernels, fused(): pl.pallas_call(kernel, out_shape=[jax.ShapeDtypeStruct(inputs.shape, BF16...  35.3 us
    pallas_call x1, Pallas kernels, fused(): pl.pallas_call(finish, out_shape=[jax.ShapeDtypeStruct(inputs.shape, BF16...  2.24 us

profile of v5, /device:TPU:0, one launch (start us, length us, event | category | flops | bytes accessed | tf_op | source)
XLA Modules:
  0.0 38.2 jit_solution(8085435227249267446)
XLA Ops:
  0.6 35.3 %shard_map.93 = (bf16[2,512,512]{2,1,0:T(8,128)(2,1)}, f32[48,512]{1,0:T(8,128)}) custom-call(s32[3]{0:T(128)} %taps_ref.1, bf16[2,512,512]{2,1,0:T(8,128)(2,1)} %x_hbm.1, bf16[2,512,512]{2,1,0:T(8,128)(2,1)} %cot_hbm.1, f32[48,512]{1,0:T(8,128)} %weight.1), custom_call_target="tpu_custom_call" | custom-call | flops 4831838208 | bytes 3145728 | tf_op jit(solution)/shard_map/pallas_call | solution.py:364
  36.0 2.2 %shard_map.94 = (bf16[2,512,512]{2,1,0:T(8,128)(2,1)}, f32[48,512]{1,0:T(8,128)}, f32[48,512]{1,0:T(8,128)}, f32[48,512]{1,0:T(8,128)}) custom-call(bf16[2,512,512]{2,1,0:T(8,128)(2,1)} %get-tuple-element.6.gi, f32[48,512]{1,0:T(8,128)} %get-tuple-element.7.grad, f32[48,512]{1,0:T(8,128)} %weight.1, f32[48,512]{1,0:T(8,128)} %moment_one.1, ...), custom_call_target="tpu_custom_call" | custom-call | flops 491520 | bytes 688128 | tf_op jit(solution)/shard_map/pallas_call | solution.py:392

commit v6 on v5

--- a/solution.py
+++ b/solution.py
@@ -208,18 +208,18 @@
     loads[2].start()
     shift(0)
     first_hop(2)
+    transpose(0, 0)
+    first_hop(3)
     second_hop(0)
     shift(1)
-    first_hop(3)
     second_hop(1)
-    transpose(0, 0)
+    transpose(0, 1)
+    forward(0)
     second_hop(2)
-    forward(0)
-    transpose(0, 1)
+    transpose(1, 0)
+    forward(1)
     second_hop(3)
-    transpose(1, 0)
     transpose(1, 1)
-    forward(1)
     forward(2)
     loads[2].wait()
     for c in c_in[3]:
@@ -275,20 +275,26 @@
     def shift_dpre(s):
         first = s * time_n
         dk[1, pl.ds(first, time_n), :] = matmul(ahead, dk[0, pl.ds(first, time_n), :]).astype(BF16)
+
+    def static_shift_dpre(s):
+        first = s * time_n
         dk[2, pl.ds(first, time_n - span), :] = dk[0, pl.ds(first + span, time_n - span), :]
         dk[2, pl.ds(first + time_n - span, span), :] = jnp.zeros((span, width), BF16)
 
-    def grad_input(i):
-        size = time_n // 2
-        s, first = i // 2, (i % 2) * size
-        total = cot[s, pl.ds(first, size), :].astype(F32)
-        for k in range(3):
-            total = total + matmul_t(dk[k, pl.ds(i * size, size), :], wide[taps_at[k], :])
-        gi[s, pl.ds(first, size), :] = total.astype(BF16)
-        part = (s, pl.ds(first, size))
-        c = pltpu.make_async_copy(gi.at[part], gi_hbm.at[part], store_sem.at[i])
-        c.start()
-        stores.append(c)
+    def grad_input(k):
+        term = matmul_t(dk[k], wide[taps_at[k], :])
+        for s in range(series_n):
+            part = pl.ds(s * time_n, time_n)
+            mine = term[s * time_n : (s + 1) * time_n]
+            if k == 0:
+                pre[part, :] = cot[s].astype(F32) + mine
+            elif k == 2:
+                pre[part, :] = pre[part, :] + mine
+            else:
+                gi[s] = (pre[part, :] + mine).astype(BF16)
+                c = pltpu.make_async_copy(gi.at[s], gi_hbm.at[s], store_sem.at[s])
+                c.start()
+                stores.append(c)
 
     o = (2, 1, 3, 0)
     weight_grad(o[0])
@@ -299,22 +305,23 @@
     weight_grad(o[3])
     reduce_one(o[2])
     reduce_one(o[3])
-    shift_dpre(0)
+    grad_input(0)
     reduce_two(o[0])
-    grad_input(0)
+    for s in range(series_n):
+        static_shift_dpre(s)
+    grad_input(2)
     reduce_two(o[1])
+    for s in range(series_n):
+        shift_dpre(s)
+    reduce_two(o[2])
+    reduce_two(o[3])
     grad_input(1)
-    reduce_two(o[2])
-    shift_dpre(1)
-    reduce_two(o[3])
-    grad_input(2)
-    grad_input(3)
     total = grad_ref[...]
     for d in (2, 1, 3):
         z4[d].wait_recv()
         total = total + r3[d - 1].astype(F32)
     grad_ref[...] = total
-    c = pltpu.make_async_copy(grad_ref, grad_hbm, store_sem.at[2 * series_n])
+    c = pltpu.make_async_copy(grad_ref, grad_hbm, store_sem.at[series_n])
     c.start()
     stores.append(c)
     for c in z_in[1:] + sum(p_in, []) + sum(c_in, []) + sum(p2.values(), []):
@@ -378,7 +385,7 @@
             V((PLANES, 4, rows, width), BF16), V((PLANES, 4, rows, width), BF16),
             V((PLANES, 3, rows, width), BF16), V((PLANES, 3, rows, width), BF16),
             V((3, rows, width), BF16), V((3, rows, width), BF16),
-            pltpu.SemaphoreType.DMA((3,)), pltpu.SemaphoreType.DMA((2 * series_n + 1,)),
+            pltpu.SemaphoreType.DMA((3,)), pltpu.SemaphoreType.DMA((series_n + 1,)),
             pltpu.SemaphoreType.DMA((32,)), pltpu.SemaphoreType.DMA((32,)),
             pltpu.SemaphoreType.DMA((19,)), pltpu.SemaphoreType.DMA((19,)),
         ],

time: 38.4 us -> 37.9 us (0.987)
  Pallas kernels: 37.6 us -> 37.1 us
    pallas_call x1, Pallas kernels: 35.3 us -> 34.9 us  [fused(): pl.pallas_call(kernel, out_shape=[jax.ShapeDtypeStruct(inputs.shape, BF16...]
where the time goes in v6:
time: 37.9 us; the launch traced here: 37.8 us
  Pallas kernels  37.1 us (98%)
  between operations  0.64 us (2%)
    pallas_call x1, Pallas kernels, fused(): pl.pallas_call(kernel, out_shape=[jax.ShapeDtypeStruct(inputs.shape, BF16...  34.9 us
    pallas_call x1, Pallas kernels, fused(): pl.pallas_call(finish, out_shape=[jax.ShapeDtypeStruct(inputs.shape, BF16...  2.24 us

profile of v6, /device:TPU:0, one launch (start us, length us, event | category | flops | bytes accessed | tf_op | source)
XLA Modules:
  0.0 37.8 jit_solution(670271572292509945)
XLA Ops:
  0.6 34.9 %shard_map.93 = (bf16[2,512,512]{2,1,0:T(8,128)(2,1)}, f32[48,512]{1,0:T(8,128)}) custom-call(s32[3]{0:T(128)} %taps_ref.1, bf16[2,512,512]{2,1,0:T(8,128)(2,1)} %x_hbm.1, bf16[2,512,512]{2,1,0:T(8,128)(2,1)} %cot_hbm.1, f32[48,512]{1,0:T(8,128)} %weight.1), custom_call_target="tpu_custom_call" | custom-call | flops 4831838208 | bytes 3145728 | tf_op jit(solution)/shard_map/pallas_call | solution.py:371
  35.5 2.2 %shard_map.94 = (bf16[2,512,512]{2,1,0:T(8,128)(2,1)}, f32[48,512]{1,0:T(8,128)}, f32[48,512]{1,0:T(8,128)}, f32[48,512]{1,0:T(8,128)}) custom-call(bf16[2,512,512]{2,1,0:T(8,128)(2,1)} %get-tuple-element.6.gi, f32[48,512]{1,0:T(8,128)} %get-tuple-element.7.grad, f32[48,512]{1,0:T(8,128)} %weight.1, f32[48,512]{1,0:T(8,128)} %moment_one.1, ...), custom_call_target="tpu_custom_call" | custom-call | flops 491520 | bytes 688128 | tf_op jit(solution)/shard_map/pallas_call | solution.py:399

commit v7 on v6

--- a/solution.py
+++ b/solution.py
@@ -198,7 +198,7 @@
         at = pl.ds(first, time_n)
         turned = x[s, :, pl.ds(h * half, half)].T
         xt[pl.ds(h * half, half), at] = turned
-        xt[pl.ds(width + h * half, half), at] = matmul(turned, ahead).astype(BF16)
+        xt[pl.ds(width + h * half, half), at] = xs[at, pl.ds(width + h * half, half)].T
         last = pl.ds(2 * width + h * half, half)
         xt[last, pl.ds(first, span)] = jnp.zeros((half, span), BF16)
         xt[last, pl.ds(first + span, time_n - span)] = turned[:, : time_n - span]

time: 37.9 us -> 37.7 us (level)
  no operation moved by 1% of the time
where the time goes in v7:
time: 37.7 us; the launch traced here: 37.5 us
  Pallas kernels  36.9 us (98%)
  between operations  0.64 us (2%)
    pallas_call x1, Pallas kernels, fused(): pl.pallas_call(kernel, out_shape=[jax.ShapeDtypeStruct(inputs.shape, BF16...  34.7 us
    pallas_call x1, Pallas kernels, fused(): pl.pallas_call(finish, out_shape=[jax.ShapeDtypeStruct(inputs.shape, BF16...  2.24 us

profile of v7, /device:TPU:0, one launch (start us, length us, event | category | flops | bytes accessed | tf_op | source)
XLA Modules:
  0.0 37.5 jit_solution(10150656734373153433)
XLA Ops:
  0.6 34.7 %shard_map.93 = (bf16[2,512,512]{2,1,0:T(8,128)(2,1)}, f32[48,512]{1,0:T(8,128)}) custom-call(s32[3]{0:T(128)} %taps_ref.1, bf16[2,512,512]{2,1,0:T(8,128)(2,1)} %x_hbm.1, bf16[2,512,512]{2,1,0:T(8,128)(2,1)} %cot_hbm.1, f32[48,512]{1,0:T(8,128)} %weight.1), custom_call_target="tpu_custom_call" | custom-call | flops 4831838208 | bytes 3145728 | tf_op jit(solution)/shard_map/pallas_call | solution.py:371
  35.3 2.2 %shard_map.94 = (bf16[2,512,512]{2,1,0:T(8,128)(2,1)}, f32[48,512]{1,0:T(8,128)}, f32[48,512]{1,0:T(8,128)}, f32[48,512]{1,0:T(8,128)}) custom-call(bf16[2,512,512]{2,1,0:T(8,128)(2,1)} %get-tuple-element.6.gi, f32[48,512]{1,0:T(8,128)} %get-tuple-element.7.grad, f32[48,512]{1,0:T(8,128)} %weight.1, f32[48,512]{1,0:T(8,128)} %moment_one.1, ...), custom_call_target="tpu_custom_call" | custom-call | flops 491520 | bytes 688128 | tf_op jit(solution)/shard_map/pallas_call | solution.py:399
